TPU v7x, 32 devices: a whole 2x2x4 slice. The times are simulated.
32 devices in a mesh: dp: 4 (over y, x), mp: 4 (over z), outer: 2 (over core).
Axes of the slice: x: 2, y: 2, z: 4, core: 2. Of those that a mesh axis runs over, the one named last changes fastest.
Arguments:
- activations: bfloat16 [16384, 8192], P(('dp', 'outer'), 'mp'), may hold values from -6 to 6
- act_scale: float32 [128, 64], P(('dp', 'outer'), 'mp'), may hold values from 0.25 to 4
- out_grads: bfloat16 [16384, 16384], P(('dp', 'outer'), 'mp'), may hold values from -6 to 6
- gradient_tile_scale: float32 [128, 128], P(('dp', 'outer'), 'mp'), may hold values from 0.25 to 4
- prior_input_factor: float32 [8, 1024, 1024], P('mp', ('dp', 'outer')), may hold values from -0.3 to 6, as said below
- g_factor: float32 [16, 1024, 1024], P('mp', ('dp', 'outer')), may hold values from -0.3 to 6, as said below
- weight_grad: bfloat16 [8192, 16384], P('mp', ('dp', 'outer')), may hold values from -6 to 6
- a_inverse: bfloat16 [8, 1024, 1024], P('mp', ('dp', 'outer')), as said below
- g_inverse: bfloat16 [16, 1024, 1024], P(('dp', 'outer'), 'mp'), as said below
Outputs:
- a_stat: float32 [8, 1024, 1024], P('mp', ('dp', 'outer'))
- g_stat: float32 [16, 1024, 1024], P('mp', ('dp', 'outer'))
- new_a_factor: float32 [8, 1024, 1024], P('mp', ('dp', 'outer'))
- new_g_factor: float32 [16, 1024, 1024], P('mp', ('dp', 'outer'))
- preconditioned: bfloat16 [8192, 16384], P('mp', ('dp', 'outer'))
Inputs may be any that keep to these rules, and one draw needn't show every extreme that they name: `a_inverse`: each block is the identity plus dense off-diagonal and diagonal entries of magnitude at most 1.5 / sqrt(1024). `g_inverse`: each block is the identity plus dense off-diagonal and diagonal entries of magnitude at most 1.5 / sqrt(1024). `prior_input_factor`: each block is symmetric with a positive diagonal. `g_factor`: each block is symmetric with a positive diagonal.
All inputs are finite; a program needn't handle non-finite values.
Results may differ from a plain program's by a relative error of at most 0.014.
Values may be sent and summed in bfloat16 or wider, within the bound.
No kernel may reach another device: no remote copies, remote signals or barrier semaphores. Data moves between devices by JAX's collectives and lax.ppermute only.
A program may use at most 128 MiB of HBM per device.

v0:
```python
import jax
import jax.numpy as jnp
from jax import lax
from jax.sharding import PartitionSpec as P

BLK = 1024
QT = 128


EMA_DECAY = 0.95


def dequantize(quantized, tile_scale):
    row_total, column_total = quantized.shape
    tiles_with_scale = (
        quantized.reshape(row_total // QT, QT, column_total // QT, QT)
        * tile_scale[:, None, :, None]
    )
    return tiles_with_scale.reshape(row_total, column_total).astype(jnp.bfloat16)


def body(
    activations,
    act_scale,
    out_grads,
    gradient_tile_scale,
    prior_input_factor,
    g_factor,
    weight_grad,
    a_inverse,
    g_inverse,
):
    input_factor_tiles = dequantize(activations, act_scale).reshape(activations.shape[0], -1, BLK)
    gradient_factor_tiles = dequantize(out_grads, gradient_tile_scale).reshape(
        out_grads.shape[0], -1, BLK
    )
    input_count = input_factor_tiles.shape[1]
    activation_rows = jnp.einsum(
        "qym,qyx->myx", input_factor_tiles, input_factor_tiles, preferred_element_type=jnp.float32
    )
    gradient_rows = jnp.einsum(
        "qym,qyx->myx",
        gradient_factor_tiles,
        gradient_factor_tiles,
        preferred_element_type=jnp.float32,
    )
    summed = lax.psum_scatter(
        jnp.concatenate([activation_rows, gradient_rows], axis=1).astype(jnp.bfloat16),
        ("dp", "outer"),
        scatter_dimension=0,
        tiled=True,
    ).astype(jnp.float32)
    token_total = activations.shape[0] * lax.axis_size("dp") * lax.axis_size("outer")
    statistics = jnp.transpose(summed, (1, 0, 2)) / token_total
    a_stat = statistics[:input_count]
    g_stat = statistics[input_count:]
    new_a_factor = EMA_DECAY * prior_input_factor + (1.0 - EMA_DECAY) * a_stat
    new_g_factor = EMA_DECAY * g_factor + (1.0 - EMA_DECAY) * g_stat
    row_blocks = weight_grad.shape[0] // BLK
    column_blocks = weight_grad.shape[1] // BLK
    grad_blocks = weight_grad.reshape(row_blocks, BLK, column_blocks, BLK)
    right = jnp.einsum(
        "aigk,gkl->aigl",
        grad_blocks,
        lax.all_gather(g_inverse, "mp", axis=1, tiled=True),
        preferred_element_type=jnp.float32,
    ).astype(jnp.bfloat16)
    result = jnp.einsum(
        "aij,ajgl->aigl",
        lax.all_gather(a_inverse, ("dp", "outer"), axis=1, tiled=True),
        right,
        preferred_element_type=jnp.float32,
    ).astype(jnp.bfloat16)
    return (
        a_stat,
        g_stat,
        new_a_factor,
        new_g_factor,
        result.reshape(row_blocks * BLK, column_blocks * BLK),
    )


def solution(mesh):
    return jax.shard_map(
        body,
        mesh=mesh,
        in_specs=(
            P(("dp", "outer"), "mp"),
            P(("dp", "outer"), "mp"),
            P(("dp", "outer"), "mp"),
            P(("dp", "outer"), "mp"),
            P("mp", ("dp", "outer"), None),
            P("mp", ("dp", "outer"), None),
            P("mp", ("dp", "outer")),
            P("mp", ("dp", "outer"), None),
            P(("dp", "outer"), "mp", None),
        ),
        out_specs=(
            P("mp", ("dp", "outer"), None),
            P("mp", ("dp", "outer"), None),
            P("mp", ("dp", "outer"), None),
            P("mp", ("dp", "outer"), None),
            P("mp", ("dp", "outer")),
        ),
        check_vma=False,
    )
```

profile of v0, /device:TPU:8, one launch (start us, length us, event | category | flops | bytes accessed | tf_op | source)
XLA Modules:
  0.0 252.9 jit_solution(4480398758486913476)
XLA Ops:
  7.2 0.0 all-gather.3.cloned.1.call-start
  7.2 2.3 copy.41
  9.5 0.0 all-gather.3.cloned.1.call-update
  9.5 0.0 all-gather.5.cloned.1.call-start
  9.5 0.7 all-gather.5.cloned.1.call-update
  10.3 0.0 reduce-scatter.4.cloned.1.call-start
  10.3 1.8 mul.46
  12.1 11.8 %fusion.1 = bf16[2048,2048]{1,0:T(8,128)(2,1)} fusion(f32[256,8,16,128]{3,2,1,0:T(8,128)S(1)} %bitcast.56, bf16[2048,2048]{1,0:T(8,128)(2,1)} %param.9), kind=kLoop, calls=%fused_computation.3 | loop fusion | flops 12582912 | bytes 33554432 | tf_op jit(solution)/shard_map/convert_element_type | solution.py:19
  24.0 0.0 copy-start.2
  24.0 15.2 %convert_bitcast_fusion.2 = bf16[1024,2,1024]{0,2,1:T(8,128)(2,1)} fusion(bf16[256,2,8,1024]{3,2,1,0:T(8,128)(2,1)} %bitcast.61), kind=kOutput, calls=%fused_computation.20 | convolution fusion | flops 8592031744 | bytes 12582912 | tf_op jit(solution)/shard_map/qym,qyx->myx/dot_general | solution.py:38
  39.1 0.0 copy-done.2
  39.1 4.9 %mul.49 = f32[16,128,32,128]{3,2,1,0:T(8,128)S(1)} broadcast(f32[16,32]{1,0:T(8,128)S(1)} %copy-done.2), dimensions={0,2} | broadcast | bytes 33556480 | tf_op jit(solution)/shard_map/mul | solution.py:16
  44.0 26.9 %fusion = bf16[2048,4096]{1,0:T(8,128)(2,1)} fusion(f32[256,8,32,128]{3,2,1,0:T(8,128)S(1)} %bitcast.55, bf16[2048,4096]{1,0:T(8,128)(2,1)} %param.11), kind=kLoop, calls=%fused_computation.1 | loop fusion | flops 25165824 | bytes 67108864 | tf_op jit(solution)/shard_map/convert_element_type | solution.py:19
  70.9 26.6 %convert_bitcast_fusion.1 = bf16[1024,4,1024]{0,2,1:T(8,128)(2,1)} fusion(bf16[256,4,8,1024]{3,2,1,0:T(8,128)(2,1)} %bitcast.59), kind=kOutput, calls=%fused_computation.17 | convolution fusion | flops 17184063488 | bytes 25165824 | tf_op jit(solution)/shard_map/qym,qyx->myx/dot_general | solution.py:41
  97.5 10.6 %pad_maximum_fusion = bf16[1024,6,1024]{0,2,1:T(8,128)(2,1)} fusion(bf16[1024,4,1024]{0,2,1:T(8,128)(2,1)} %convert_bitcast_fusion.1, bf16[1024,2,1024]{0,2,1:T(8,128)(2,1)} %convert_bitcast_fusion.2), kind=kLoop, calls=%fused_computation.7 | loop fusion | flops 6291456 | bytes 25165824 | tf_op jit(solution)/shard_map/concatenate | solution.py:48
  108.1 16.7 %copy.51 = bf16[1024,6144]{1,0:T(8,128)(2,1)} copy(bf16[1024,6144]{0,1:T(8,128)(2,1)} %bitcast.57) | data formatting | bytes 25165824
  124.8 0.0 copy-start
  124.8 0.0 copy-start.1
  124.8 0.0 reduce-scatter.4.cloned.1.call-update
  124.9 1.6 copy-done
  126.5 1.8 copy.40
  128.3 0.0 copy-done.1
  128.3 1.3 copy.39
  129.6 14.8 %reshape.32 = bf16[2,1024,2,1024]{3,2,1,0:T(2,128)(2,1)} reshape(bf16[2048,2048]{1,0:T(8,128)(2,1)} %param.15) | data formatting | bytes 16777216 | tf_op jit(solution)/shard_map/reshape | solution.py:61
  144.4 0.0 all-gather.3.cloned.1.call-done
  144.4 0.0 all-gather.5.cloned.1.call-done
  144.4 27.0 %convert_bitcast_fusion = bf16[2,1024,2,1024]{1,3,2,0:T(8,128)(2,1)} fusion(bf16[2,1024,1024]{2,1,0:T(8,128)(2,1)} %all-gather.5.cloned.1.call-done, bf16[2,1024,2,1024]{3,2,1,0:T(2,128)(2,1)} %reshape.32, bf16[2,1024,1024]{1,2,0:T(8,128)(2,1)} %all-gather.3.cloned.1.call-done), kind=kOutput, calls=%fused_computation.15 | convolution fusion | flops 17188257792 | bytes 25165824 | tf_op jit(solution)/shard_map/aij,ajgl->aigl/dot_general | solution.py:68
  171.4 21.7 %copy.43 = bf16[2,1024,2,1024]{3,2,1,0:T(2,128)(2,1)} copy(bf16[2,1024,2,1024]{1,3,2,0:T(8,128)(2,1)} %convert_bitcast_fusion) | data formatting | bytes 16777216 | tf_op jit(solution)/shard_map/convert_element_type | solution.py:73
  193.1 10.4 %copy.57 = bf16[256,8,2,1024]{3,1,2,0:T(8,128)(2,1)} copy(bf16[256,8,2,1024]{3,2,1,0:T(2,128)(2,1)} %bitcast.58) | data formatting | bytes 16777216
  203.5 21.1 %reduce-scatter.4.cloned.1.call-done = bf16[128,6144]{1,0:T(8,128)(2,1)} async-done(((bf16[1024,6144]{1,0:T(8,128)(2,1)}), bf16[128,6144]{1,0:T(8,128)(2,1)}) %reduce-scatter.4.cloned.1.call-update) | async-done | bytes 1572880
  224.7 2.6 %copy.52 = bf16[128,6144]{0,1:T(8,128)(2,1)} copy(bf16[128,6144]{1,0:T(8,128)(2,1)} %reduce-scatter.4.cloned.1.call-done) | data formatting | bytes 3145728
  227.2 1.6 multiply_bitcast_fusion
  228.9 4.0 %multiply_add_fusion = (f32[4,128,1024]{1,2,0:T(8,128)}, f32[4,128,1024]{1,2,0:T(8,128)}) fusion(f32[4,128,1024]{1,2,0:T(8,128)} %copy.40, f32[6,128,1024]{1,2,0:T(8,128)S(1)} %multiply_bitcast_fusion), kind=kLoop, calls=%fused_computation.22 | loop fusion | flops 1572864 | bytes 8388608 | tf_op jit(solution)/shard_map/add | solution.py:58
  232.8 2.9 %copy.45 = f32[4,128,1024]{2,1,0:T(8,128)} copy(f32[4,128,1024]{1,2,0:T(8,128)} %get-tuple-element.21) | data formatting | bytes 4194304
  235.7 2.9 %copy.47 = f32[4,128,1024]{2,1,0:T(8,128)} copy(f32[4,128,1024]{1,2,0:T(8,128)} %get-tuple-element.20) | data formatting | bytes 4194304
  238.6 2.7 %multiply_add_fusion.1 = (f32[2,128,1024]{1,2,0:T(8,128)}, f32[2,128,1024]{1,2,0:T(8,128)}) fusion(f32[2,128,1024]{1,2,0:T(8,128)} %copy.39, f32[6,128,1024]{1,2,0:T(8,128)S(1)} %multiply_bitcast_fusion), kind=kLoop, calls=%fused_computation.23 | loop fusion | flops 786432 | bytes 4194304 | tf_op jit(solution)/shard_map/add | solution.py:57
  241.3 2.5 %copy.44 = f32[2,128,1024]{2,1,0:T(8,128)} copy(f32[2,128,1024]{1,2,0:T(8,128)} %get-tuple-element.23) | data formatting | bytes 2097152
  243.8 2.5 %copy.46 = f32[2,128,1024]{2,1,0:T(8,128)} copy(f32[2,128,1024]{1,2,0:T(8,128)} %get-tuple-element.22) | data formatting | bytes 2097152
Async XLA Ops:
  7.2 137.3 %all-gather.3.cloned.1.call-start = ((), (), s32[]{:S(2)}) async-start(), calls=%async_computation.1 | async-start | bytes 5242880 | tf_op jit(solution)/shard_map/all_gather | solution.py:65
  9.5 134.9 %all-gather.5.cloned.1.call-start = ((), (), s32[]{:S(2)}) async-start(), calls=%async_computation.2 | async-start | bytes 4718592 | tf_op jit(solution)/shard_map/all_gather | solution.py:70
  10.3 214.4 %reduce-scatter.4.cloned.1.call-start = ((), (), s32[]{:S(2)}) async-start(), calls=%async_computation.3 | async-start | bytes 14155776
  24.0 15.2 %copy-start.2 = (f32[16,32]{1,0:T(8,128)S(1)}, f32[16,32]{1,0:T(8,128)}, u32[]{:S(2)}) copy-start(f32[16,32]{1,0:T(8,128)} %param.12) | copy-start | bytes 6148
  124.8 1.7 copy-start
  124.8 3.5 %copy-start.1 = (f32[2,128,1024]{2,1,0:T(8,128)S(1)}, f32[2,128,1024]{2,1,0:T(8,128)}, u32[]{:S(2)}) copy-start(f32[2,128,1024]{2,1,0:T(8,128)} %param.13) | copy-start | bytes 3145732
Sparse Core Ops, SparseCore 0:
  10.1 78.7 all-gather.2
  90.8 37.8 all-gather.4
  132.2 92.3 reduce-scatter.3
where the time goes:
time: 256 us; the launch traced here: 253 us
  local copies, waits for them, and re-layouts  90.8 us (35%)
  matrix products  68.7 us (27%)
  other arithmetic  57.6 us (22%)
  waiting for transfers between devices  21.9 us (9%)
  between operations  13.8 us (5%)
    unnamed x16, local copies, waits for them, and re-layouts  47.5 us
    convert_element_type x2, other arithmetic, dequantize(): tiles_with_scale.reshape(row_total, column_total).astype(jnp.bfloat16)  38.7 us
    dot_general x1, matrix products, body(): jnp.einsum('aij,ajgl->aigl', lax.all_gather(a_inverse, ('dp', 'outer'), a...  27 us
    dot_general x1, matrix products, body(): jnp.einsum('qym,qyx->myx', gradient_factor_tiles, gradient_factor_tiles,...  26.6 us
    unnamed x4, waiting for transfers between devices  21.9 us
    convert_element_type x1, local copies, waits for them, and re-layouts, body(): result = jnp.einsum('aij,ajgl->aigl', lax.all_gather(a_inverse, ('dp', 'o...  21.7 us
    dot_general x1, matrix products, body(): jnp.einsum('qym,qyx->myx', input_factor_tiles, input_factor_tiles, prefer...  15.2 us
    reshape x1, local copies, waits for them, and re-layouts, body(): grad_blocks = weight_grad.reshape(row_blocks, BLK, column_blocks, BLK)  14.8 us
  transfers between devices with their start and end apart: 3, of which 1 were waited for; matrix products, arithmetic and copies ran while one was open for 76% of the time, Pallas kernels for 0%

commit v1 on v0

v1 whole, which is shorter than its diff:
```python
import jax
import jax.numpy as jnp
from jax import lax
from jax.experimental import pallas as pl
from jax.experimental.pallas import tpu as pltpu
from jax.sharding import PartitionSpec as P

BLK = 1024
QT = 128
EMA_DECAY = 0.95
BF = jnp.bfloat16
F32 = jnp.float32
VMEM_LIMIT = 48 * 1024 * 1024


def dequantize(quantized, tile_scale):
    rows, columns = quantized.shape
    tiles = (
        quantized.reshape(rows // QT, QT, columns // QT, QT).astype(F32)
        * tile_scale[:, None, :, None]
    )
    return tiles.reshape(rows, columns).astype(BF)


def position(chip, my_chip, bits, order):
    relative = jnp.bitwise_xor(chip, my_chip)
    place = 0
    for bit in order:
        place = place * 2 + jnp.bitwise_and(jnp.right_shift(relative, bit), 1)
    return place


def bit_order(block, bits):
    return [(block + k) % bits for k in range(bits)]


def gram_blocks(where, panel, scale, first, count, chips):
    tokens = panel.shape[0]
    bits = chips.bit_length() - 1
    pair = BLK // chips
    tile = pair // 2
    half = chips // 2
    width = tile * (chips + 1)
    tiles = BLK // QT

    def body(where_ref, scale_ref, x_ref, keep_ref, send_ref, deq):
        step = pl.program_id(0)

        def convert(t, carry):
            rows = pl.ds(pl.multiple_of(t * QT, QT), QT)
            for u in range(tiles):
                value = x_ref[rows, u * QT : (u + 1) * QT].astype(F32)
                value = (value * scale_ref[t, (first + step) * tiles + u]).astype(BF)
                deq[rows, u * QT : (u + 1) * QT] = value
                if u * QT < half * pair:
                    deq[rows, BLK + u * QT : BLK + (u + 1) * QT] = value
            return carry

        lax.fori_loop(0, tokens // QT, convert, 0, unroll=2)
        order_even = bit_order(0, bits)
        order_odd = bit_order(1, bits)
        far = []
        for chip in range(chips):
            span = half * pair + (pair if chip < half else 0)
            start = chip * pair
            sums = lax.dot_general(
                deq[:, start : start + pair],
                deq[:, start : start + span],
                (((0,), (0,)), ((), ())),
                preferred_element_type=F32,
            )
            near = sums[:, : half * pair].astype(BF)
            if chip < half:
                last = sums[:, half * pair :]
                far.append(last)
            else:
                last = jnp.transpose(far[chip - half])
            last = last.astype(BF)
            place = jnp.where(
                (first + step) % 2 == 0,
                position(chip, where_ref[0], bits, order_even),
                position(chip, where_ref[0], bits, order_odd),
            )

            def store(ref, core, near=near, last=last, place=place):
                cut = near.shape[1] - core * tile
                ref[0, place, :, :cut] = near[core * tile : (core + 1) * tile, core * tile :]
                ref[0, place, :, cut:] = last[core * tile : (core + 1) * tile, : (core + 1) * tile]

            @pl.when(where_ref[1] == 0)
            def _():
                store(keep_ref, 0)
                store(send_ref, 1)

            @pl.when(where_ref[1] == 1)
            def _():
                store(keep_ref, 1)
                store(send_ref, 0)

    shape = jax.ShapeDtypeStruct((count, chips, tile, width), BF)
    spec = pl.BlockSpec((1, chips, tile, width), lambda b: (b, 0, 0, 0))
    return pl.pallas_call(
        body,
        grid=(count,),
        out_shape=(shape, shape),
        in_specs=[
            pl.BlockSpec(memory_space=pltpu.SMEM),
            pl.BlockSpec(memory_space=pltpu.SMEM),
            pl.BlockSpec((tokens, BLK), lambda b: (0, first + b)),
        ],
        out_specs=(spec, spec),
        scratch_shapes=[pltpu.VMEM((tokens, BLK + half * pair), BF)],
        compiler_params=pltpu.CompilerParams(vmem_limit_bytes=VMEM_LIMIT),
        cost_estimate=pl.CostEstimate(
            flops=2 * count * tokens * BLK * width,
            bytes_accessed=2 * count * (tokens * BLK + 2 * chips * tile * width),
            transcendentals=0,
        ),
    )(where, scale, panel)


def swap(value, axis, size, bit):
    return lax.ppermute(value, axis, [(i, i ^ (1 << bit)) for i in range(size)])


def scatter_sums(keep, send, first, chips):
    bits = chips.bit_length() - 1
    got = lax.ppermute(send, "outer", [(0, 1), (1, 0)])
    left, right = [], []
    for b in range(keep.shape[0]):
        held, came = keep[b], got[b]
        for bit in bit_order(first + b, bits):
            size = held.shape[0] // 2
            away = (held[size:].astype(F32) + came[size:].astype(F32)).astype(BF)
            came_next = swap(away, "dp", chips, bit)
            held = (held[:size].astype(F32) + came[:size].astype(F32)).astype(BF)
            came = came_next
        left.append(held[0])
        right.append(came[0])
    return left, right


def symmetric_statistics(activations, act_scale, out_grads, gradient_tile_scale, prior_input_factor, g_factor):
    chips = lax.axis_size("dp")
    devices = 2 * chips
    tile = BLK // devices
    token_total = activations.shape[0] * devices
    where = jnp.stack([lax.axis_index("dp"), lax.axis_index("outer")]).astype(jnp.int32)
    inputs = activations.shape[1] // BLK
    hidden = out_grads.shape[1] // BLK
    left, right = [], []
    for panel, scale, total in ((out_grads, gradient_tile_scale, hidden), (activations, act_scale, inputs)):
        for first in range(0, total, 2):
            keep, send = gram_blocks(where, panel, scale, first, min(2, total - first), chips)
            some_left, some_right = scatter_sums(keep, send, first, chips)
            left += some_left
            right += some_right
    left, right = jnp.stack(left), jnp.stack(right)
    mirrored = []
    for k in range(1, chips):
        columns = slice(k * tile, (k + 1) * tile)
        sent = (left[:, :, columns].astype(F32) + right[:, :, columns].astype(F32)).astype(BF)
        mirrored.append(
            lax.ppermute(sent, ("dp", "outer"), [(i, (i + k) % devices) for i in range(devices)])
        )

    def finish(prior, low):
        count = prior.shape[0]

        def body(where_ref, prior_ref, left_ref, right_ref, *rest):
            mirror_refs, stat_ref, new_ref = rest[: chips - 1], rest[-2], rest[-1]
            me = where_ref[0] * 2 + where_ref[1]

            def put(at, sums):
                columns = pl.ds(pl.multiple_of(lax.rem(me + at, devices) * tile, tile), tile)
                stat = sums * (1.0 / token_total)
                stat_ref[0, :, columns] = stat
                new_ref[0, :, columns] = EMA_DECAY * prior_ref[0, :, columns] + (1.0 - EMA_DECAY) * stat

            for k in range(chips + 1):
                columns = slice(k * tile, (k + 1) * tile)
                put(k, left_ref[0, :, columns].astype(F32) + right_ref[0, :, columns].astype(F32))
            for k in range(1, chips):
                put(devices - k, jnp.transpose(mirror_refs[k - 1][0].astype(F32)))

        rows = pl.BlockSpec((1, tile, BLK), lambda b: (b, 0, 0))
        part = pl.BlockSpec((1, tile, tile * (chips + 1)), lambda b: (low + b, 0, 0))
        square = pl.BlockSpec((1, tile, tile), lambda b: (low + b, 0, 0))
        shape = jax.ShapeDtypeStruct((count, tile, BLK), F32)
        return pl.pallas_call(
            body,
            grid=(count,),
            out_shape=(shape, shape),
            in_specs=[pl.BlockSpec(memory_space=pltpu.SMEM), rows, part, part] + [square] * (chips - 1),
            out_specs=(rows, rows),
            compiler_params=pltpu.CompilerParams(vmem_limit_bytes=VMEM_LIMIT),
        )(where, prior, left, right, *mirrored)

    g_stat, new_g_factor = finish(g_factor, 0)
    a_stat, new_a_factor = finish(prior_input_factor, hidden)
    return a_stat, g_stat, new_a_factor, new_g_factor


def plain_statistics(activations, act_scale, out_grads, gradient_tile_scale, prior_input_factor, g_factor):
    a_tiles = dequantize(activations, act_scale).reshape(activations.shape[0], -1, BLK)
    g_tiles = dequantize(out_grads, gradient_tile_scale).reshape(out_grads.shape[0], -1, BLK)
    inputs = a_tiles.shape[1]
    tiles = jnp.concatenate([a_tiles, g_tiles], axis=1)
    rows = jnp.einsum("qym,qyx->myx", tiles, tiles, preferred_element_type=F32)
    summed = lax.psum_scatter(
        rows.astype(BF), ("dp", "outer"), scatter_dimension=0, tiled=True
    ).astype(F32)
    token_total = activations.shape[0] * lax.axis_size("dp") * lax.axis_size("outer")
    statistics = jnp.transpose(summed, (1, 0, 2)) / token_total
    a_stat, g_stat = statistics[:inputs], statistics[inputs:]
    new_a_factor = EMA_DECAY * prior_input_factor + (1.0 - EMA_DECAY) * a_stat
    new_g_factor = EMA_DECAY * g_factor + (1.0 - EMA_DECAY) * g_stat
    return a_stat, g_stat, new_a_factor, new_g_factor


def left_product(a_blocks, weight_grad):
    rows, columns = weight_grad.shape

    def body(a_ref, w_ref, o_ref):
        o_ref[...] = jnp.dot(a_ref[0], w_ref[...], preferred_element_type=F32).astype(BF)

    return pl.pallas_call(
        body,
        grid=(rows // BLK, columns // BLK),
        out_shape=jax.ShapeDtypeStruct((rows, columns), BF),
        in_specs=[
            pl.BlockSpec((1, BLK, BLK), lambda i, j: (i, 0, 0)),
            pl.BlockSpec((BLK, BLK), lambda i, j: (i, j)),
        ],
        out_specs=pl.BlockSpec((BLK, BLK), lambda i, j: (i, j)),
        compiler_params=pltpu.CompilerParams(vmem_limit_bytes=VMEM_LIMIT),
        cost_estimate=pl.CostEstimate(
            flops=2 * rows * columns * BLK,
            bytes_accessed=4 * rows * columns + 2 * rows * BLK,
            transcendentals=0,
        ),
    )(a_blocks, weight_grad)


def chain_slices(own, size):
    before, after = [own], [own]
    for hop in range(1, size):
        before.append(lax.ppermute(before[-1], "mp", [(i, i + 1) for i in range(hop - 1, size - 1)]))
        after.append(lax.ppermute(after[-1], "mp", [(i, i - 1) for i in range(1, size - hop + 1)]))
    return before, after[1:]


def right_product(me, left, before, after, block, target):
    rows, columns = left.shape
    size = len(before)
    depth = before[0].shape[0]
    height = min(512, rows)

    def body(me_ref, left_ref, *rest):
        before_refs, after_refs = rest[:size], rest[size : 2 * size - 1]
        o_ref, whole, sem = rest[-3:]

        @pl.when(pl.program_id(0) == 0)
        def _():
            mine = me_ref[0]

            def fetch(ref, owner):
                rows_of = pl.ds(pl.multiple_of(owner * depth, depth), depth)
                pltpu.make_async_copy(ref, whole.at[rows_of], sem).start()

            fetch(before_refs[0], mine)
            for hop in range(1, size):
                pl.when(mine >= hop)(lambda hop=hop: fetch(before_refs[hop], mine - hop))
                pl.when(mine + hop < size)(lambda hop=hop: fetch(after_refs[hop - 1], mine + hop))
            pltpu.make_async_copy(whole, whole, sem).wait()

        o_ref[...] = jnp.dot(left_ref[...], whole[...], preferred_element_type=F32).astype(BF)

    operands = [me, left, *before, *after]
    specs = [
        pl.BlockSpec(memory_space=pltpu.SMEM),
        pl.BlockSpec((height, BLK), lambda r: (r, block)),
    ] + [pl.BlockSpec(memory_space=pl.ANY)] * (2 * size - 1)
    aliases = {}
    if target is not None:
        aliases = {len(operands): 0}
        operands.append(target)
        specs.append(pl.BlockSpec(memory_space=pl.ANY))
    return pl.pallas_call(
        body,
        grid=(rows // height,),
        out_shape=jax.ShapeDtypeStruct((rows, columns), BF),
        in_specs=specs,
        out_specs=pl.BlockSpec((height, BLK), lambda r: (r, block)),
        scratch_shapes=[pltpu.VMEM((BLK, BLK), BF), pltpu.SemaphoreType.DMA],
        input_output_aliases=aliases,
        compiler_params=pltpu.CompilerParams(vmem_limit_bytes=VMEM_LIMIT),
        cost_estimate=pl.CostEstimate(
            flops=2 * rows * BLK * BLK,
            bytes_accessed=4 * rows * BLK + 2 * BLK * BLK,
            transcendentals=0,
        ),
    )(*operands)


def body(
    activations,
    act_scale,
    out_grads,
    gradient_tile_scale,
    prior_input_factor,
    g_factor,
    weight_grad,
    a_inverse,
    g_inverse,
):
    slices = lax.axis_size("mp")
    chains = [chain_slices(g_inverse[b], slices) for b in range(g_inverse.shape[0])]
    a_blocks = lax.all_gather(a_inverse, ("dp", "outer"), axis=1, tiled=True)
    left = left_product(a_blocks, weight_grad)

    chips = lax.axis_size("dp")
    symmetric = (
        lax.axis_size("outer") == 2
        and chips >= 2
        and chips & (chips - 1) == 0
        and BLK // (2 * chips) % QT == 0
    )
    statistics = symmetric_statistics if symmetric else plain_statistics
    stats = statistics(
        activations, act_scale, out_grads, gradient_tile_scale, prior_input_factor, g_factor
    )

    me = lax.axis_index("mp").astype(jnp.int32).reshape(1)
    result = None
    for block, (before, after) in enumerate(chains):
        result = right_product(me, left, before, after, block, result)
    return (*stats, result)


def solution(mesh):
    return jax.shard_map(
        body,
        mesh=mesh,
        in_specs=(
            P(("dp", "outer"), "mp"),
            P(("dp", "outer"), "mp"),
            P(("dp", "outer"), "mp"),
            P(("dp", "outer"), "mp"),
            P("mp", ("dp", "outer"), None),
            P("mp", ("dp", "outer"), None),
            P("mp", ("dp", "outer")),
            P("mp", ("dp", "outer"), None),
            P(("dp", "outer"), "mp", None),
        ),
        out_specs=(
            P("mp", ("dp", "outer"), None),
            P("mp", ("dp", "outer"), None),
            P("mp", ("dp", "outer"), None),
            P("mp", ("dp", "outer"), None),
            P("mp", ("dp", "outer")),
        ),
        check_vma=False,
    )
```

time: 256 us -> 202 us (0.79)
  local copies, waits for them, and re-layouts: 90.8 us -> 4.42 us
  Pallas kernels: 0 us -> 76.2 us
  matrix products: 68.7 us -> 0 us
  other arithmetic: 57.6 us -> 2.58 us
  starting transfers between devices: 0.12 us -> 51.6 us
  waiting for transfers between devices: 21.9 us -> 52.1 us
    pallas_call x0 -> x8, Pallas kernels: none -> 76.2 us  [the longest x3 39.7 us: gram_blocks(): pl.pallas_call(body, grid=(count,), out_shape=(shape, shape), in_specs=[p...]
    dot_general x3 -> x0, matrix products: 68.7 us -> none  [the longest x1 27 us: body(): jnp.einsum('aij,ajgl->aigl', lax.all_gather(a_inverse, ('dp', 'outer'), a...]
    ppermute x0 -> x30, starting transfers between devices: none -> 51.6 us  [the longest x6 21.6 us: chain_slices(): lax.ppermute(before[-1], 'mp', [(i, i + 1) for i in range(hop - 1, size -...]
    ppermute x0 -> x30, waiting for transfers between devices: none -> 51.4 us  [the longest x12 43.7 us: swap(): return lax.ppermute(value, axis, [(i, i ^ 1 << bit) for i in range(size)])]
    unnamed x16 -> x27, local copies, waits for them, and re-layouts: 47.5 us -> 4.33 us
    convert_element_type x2 -> x10, other arithmetic: 38.7 us -> 2.19 us  [the longest x3 1.03 us: scatter_sums(): held = (held[:size].astype(F32) + came[:size].astype(F32)).astype(BF)]
    convert_element_type x1 -> x0, local copies, waits for them, and re-layouts: 21.7 us -> none  [body(): result = jnp.einsum('aij,ajgl->aigl', lax.all_gather(a_inverse, ('dp', 'o...]
    unnamed x4 -> x1, waiting for transfers between devices: 21.9 us -> 0.68 us
  transfers between devices with their start and end apart: 3 -> 31, of which waited for: 1 -> 10; matrix products, arithmetic and copies ran while one was open for 76% -> 1% of each run, Pallas kernels for 0% -> 33%
where the time goes in v1:
time: 202 us; the launch traced here: 201 us
  Pallas kernels  76.2 us (38%)
  waiting for transfers between devices  52.1 us (26%)
  starting transfers between devices  51.6 us (26%)
  between operations  14.4 us (7%)
  local copies, waits for them, and re-layouts  4.42 us (2%)
  other arithmetic  2.58 us (1%)
    ppermute x12, waiting for transfers between devices, swap(): return lax.ppermute(value, axis, [(i, i ^ 1 << bit) for i in range(size)])  43.7 us
    pallas_call x3, Pallas kernels, gram_blocks(): pl.pallas_call(body, grid=(count,), out_shape=(shape, shape), in_specs=[p...  39.7 us
    ppermute x6, starting transfers between devices, chain_slices(): lax.ppermute(before[-1], 'mp', [(i, i + 1) for i in range(hop - 1, size -...  21.6 us
    pallas_call x2, Pallas kernels, right_product(): pl.pallas_call(body, grid=(rows // height,), out_shape=jax.ShapeDtypeStru...  18.1 us
    ppermute x12, starting transfers between devices, swap(): return lax.ppermute(value, axis, [(i, i ^ 1 << bit) for i in range(size)])  14.9 us
    ppermute x6, starting transfers between devices, chain_slices(): lax.ppermute(after[-1], 'mp', [(i, i - 1) for i in range(1, size - hop +...  12.5 us
    pallas_call x1, Pallas kernels, left_product(): pl.pallas_call(body, grid=(rows // BLK, columns // BLK), out_shape=jax.Sh...  12.4 us
    ppermute x3, waiting for transfers between devices, symmetric_statistics(): lax.ppermute(sent, ('dp', 'outer'), [(i, (i + k) % devices) for i in rang...  6.58 us
  transfers between devices with their start and end apart: 31, of which 10 were waited for; matrix products, arithmetic and copies ran while one was open for 1% of the time, Pallas kernels for 33%

profile of v1, /device:TPU:8, one launch (start us, length us, event | category | flops | bytes accessed | tf_op | source)
XLA Modules:
  0.0 201.4 jit_solution(4265737855871972312)
XLA Ops:
  7.2 0.0 all-gather.2.cloned.1.call-start
  7.2 0.7 all-gather.2.cloned.1.call-update
  7.9 0.1 pad_add_fusion.where_ref
  8.0 0.7 copy-done.8
  8.7 13.2 %shard_map.128 = (bf16[2,4,128,640]{3,2,1,0:T(8,128)(2,1)S(1)}, bf16[2,4,128,640]{3,2,1,0:T(8,128)(2,1)S(1)}) custom-call(s32[2]{0:T(128)S(1)} %pad_add_fusion.where_ref, f32[16,32]{1,0:T(8,128)S(1)} %copy-done.8, bf16[2048,4096]{1,0:T(8,128)(2,1)} %x_ref.4), custom_call_target="tpu_custom_call" | custom-call | flops 5368709120 | bytes 11010048 | tf_op jit(solution)/shard_map/pallas_call | solution.py:102
  21.9 0.1 collective-permute-start
  22.0 13.2 %shard_map.130 = (bf16[2,4,128,640]{3,2,1,0:T(8,128)(2,1)S(1)}, bf16[2,4,128,640]{3,2,1,0:T(8,128)(2,1)S(1)}) custom-call(s32[2]{0:T(128)S(1)} %pad_add_fusion.where_ref, f32[16,16]{1,0:T(8,128)S(1)} %copy-done.7, bf16[2048,2048]{1,0:T(8,128)(2,1)} %x_ref.5), custom_call_target="tpu_custom_call" | custom-call | flops 5368709120 | bytes 11010048 | tf_op jit(solution)/shard_map/pallas_call | solution.py:102
  35.3 0.5 collective-permute-start.6
  35.8 13.2 %shard_map.129 = (bf16[2,4,128,640]{3,2,1,0:T(8,128)(2,1)S(1)}, bf16[2,4,128,640]{3,2,1,0:T(8,128)(2,1)S(1)}) custom-call(s32[2]{0:T(128)S(1)} %pad_add_fusion.where_ref, f32[16,32]{1,0:T(8,128)S(1)} %copy-done.9, bf16[2048,4096]{1,0:T(8,128)(2,1)} %x_ref.4), custom_call_target="tpu_custom_call" | custom-call | flops 5368709120 | bytes 11010048 | tf_op jit(solution)/shard_map/pallas_call | solution.py:102
  49.0 0.2 collective-permute-start.3
  49.2 0.1 slice_bitcast_fusion
  49.3 1.9 collective-permute-start.27
  51.2 4.0 %collective-permute-start.24 = (bf16[256,1024]{1,0:T(8,128)(2,1)S(1)}, bf16[256,1024]{1,0:T(8,128)(2,1)S(1)}, u32[]{:S(2)}, u32[]{:S(2)}) collective-permute-start(bf16[256,1024]{1,0:T(8,128)(2,1)S(1)} %get-tuple-element.40.rest_0_), channel_id=1, source_target_pairs={{0,2},{2,4},{4,6},{1,3},{3,5},{5,7},{8,10},{10,12},{12,14},{9,11},... | collective-permute-start | bytes 1572872 | tf_op jit(solution)/shard_map/ppermute | solution.py:248
  55.2 1.9 collective-permute-start.21
  57.2 0.3 add_convert_fusion.9
  57.5 2.0 collective-permute-start.1
  59.5 0.3 add_convert_fusion.1
  59.9 3.6 %collective-permute-start.18 = (bf16[256,1024]{1,0:T(8,128)(2,1)S(1)}, bf16[256,1024]{1,0:T(8,128)(2,1)}, u32[]{:S(2)}, u32[]{:S(2)}) collective-permute-start(bf16[256,1024]{1,0:T(8,128)(2,1)S(1)} %get-tuple-element.41.rest_0_), channel_id=1, source_target_pairs={{0,2},{2,4},{4,6},{1,3},{3,5},{5,7},{8,10},{10,12},{12,14},{9,11},... | collective-permute-start | bytes 1572872 | tf_op jit(solution)/shard_map/ppermute | solution.py:248
  63.5 0.3 add_convert_fusion.5
  63.9 3.1 %collective-permute-done.1 = bf16[2,128,640]{2,1,0:T(8,128)(2,1)S(1)} collective-permute-done((bf16[2,128,640]{2,1,0:T(8,128)(2,1)S(1)}, bf16[2,128,640]{2,1,0:T(8,128)(2,1)S(1)}, u32[]{:S(2)}, u32[]{:S(2)}) %collective-permute-start.1) | collective-permute-done | bytes 327712 | tf_op jit(solution)/shard_map/ppermute | solution.py:123
  67.0 1.7 collective-permute-start.2
  68.8 6.7 %collective-permute-done.2 = bf16[2,128,640]{2,1,0:T(8,128)(2,1)S(1)} collective-permute-done((bf16[2,128,640]{2,1,0:T(8,128)(2,1)S(1)}, bf16[2,128,640]{2,1,0:T(8,128)(2,1)S(1)}, u32[]{:S(2)}, u32[]{:S(2)}) %collective-permute-start.2) | collective-permute-done | bytes 327712 | tf_op jit(solution)/shard_map/ppermute | solution.py:123
  75.6 1.3 collective-permute-start.4
  76.9 0.1 fusion.19
  77.0 6.3 %collective-permute-done.4 = bf16[2,128,640]{2,1,0:T(8,128)(2,1)S(1)} collective-permute-done((bf16[2,128,640]{2,1,0:T(8,128)(2,1)S(1)}, bf16[2,128,640]{2,1,0:T(8,128)(2,1)S(1)}, u32[]{:S(2)}, u32[]{:S(2)}) %collective-permute-start.4) | collective-permute-done | bytes 327712 | tf_op jit(solution)/shard_map/ppermute | solution.py:123
  83.3 1.1 collective-permute-start.5
  84.4 0.1 fusion.20
  84.5 5.9 %collective-permute-done.5 = bf16[2,128,640]{2,1,0:T(8,128)(2,1)S(1)} collective-permute-done((bf16[2,128,640]{2,1,0:T(8,128)(2,1)S(1)}, bf16[2,128,640]{2,1,0:T(8,128)(2,1)S(1)}, u32[]{:S(2)}, u32[]{:S(2)}) %collective-permute-start.5) | collective-permute-done | bytes 327712 | tf_op jit(solution)/shard_map/ppermute | solution.py:123
  90.4 1.0 collective-permute-start.7
  91.4 0.1 fusion.21
  91.5 6.0 %collective-permute-done.7 = bf16[2,128,640]{2,1,0:T(8,128)(2,1)S(1)} collective-permute-done((bf16[2,128,640]{2,1,0:T(8,128)(2,1)S(1)}, bf16[2,128,640]{2,1,0:T(8,128)(2,1)S(1)}, u32[]{:S(2)}, u32[]{:S(2)}) %collective-permute-start.7) | collective-permute-done | bytes 327712 | tf_op jit(solution)/shard_map/ppermute | solution.py:123
  97.4 1.1 collective-permute-start.8
  98.5 0.1 fusion.22
  98.6 7.7 %collective-permute-done.8 = bf16[2,128,640]{2,1,0:T(8,128)(2,1)S(1)} collective-permute-done((bf16[2,128,640]{2,1,0:T(8,128)(2,1)S(1)}, bf16[2,128,640]{2,1,0:T(8,128)(2,1)S(1)}, u32[]{:S(2)}, u32[]{:S(2)}) %collective-permute-start.8) | collective-permute-done | bytes 327712 | tf_op jit(solution)/shard_map/ppermute | solution.py:123
  106.3 1.0 collective-permute-start.10
  107.3 1.5 collective-permute-start.9
  108.9 0.1 fusion.23.left_ref
  108.9 4.9 %collective-permute-done.9 = bf16[1,128,640]{2,1,0:T(8,128)(2,1)S(1)} collective-permute-done((bf16[1,128,640]{2,1,0:T(8,128)(2,1)S(1)}, bf16[1,128,640]{2,1,0:T(8,128)(2,1)S(1)}, u32[]{:S(2)}, u32[]{:S(2)}) %collective-permute-start.9) | collective-permute-done | bytes 163872 | tf_op jit(solution)/shard_map/ppermute | solution.py:123
  113.8 1.4 collective-permute-start.11
  115.2 0.7 collective-permute-start.12
  116.0 3.1 %collective-permute-done.11 = bf16[1,128,640]{2,1,0:T(8,128)(2,1)S(1)} collective-permute-done((bf16[1,128,640]{2,1,0:T(8,128)(2,1)S(1)}, bf16[1,128,640]{2,1,0:T(8,128)(2,1)S(1)}, u32[]{:S(2)}, u32[]{:S(2)}) %collective-permute-start.11) | collective-permute-done | bytes 163872 | tf_op jit(solution)/shard_map/ppermute | solution.py:123
  119.1 1.4 collective-permute-start.13
  120.5 1.9 collective-permute-start.28
  122.5 5.5 %collective-permute-start.25 = (bf16[256,1024]{1,0:T(8,128)(2,1)S(1)}, bf16[256,1024]{1,0:T(8,128)(2,1)}, u32[]{:S(2)}, u32[]{:S(2)}) collective-permute-start(bf16[256,1024]{1,0:T(8,128)(2,1)S(1)} %collective-permute-done.24.rest_1_), channel_id=1, source_target_pairs={{2,4},{4,6},{3,5},{5,7},{10,12},{12,14},{11,13},{13,15},{18,20},{2... | collective-permute-start | bytes 1572872 | tf_op jit(solution)/shard_map/ppermute | solution.py:248
  128.0 0.7 collective-permute-start.14
  128.7 1.9 collective-permute-start.22
  130.7 5.5 %collective-permute-start.19 = (bf16[256,1024]{1,0:T(8,128)(2,1)}, bf16[256,1024]{1,0:T(8,128)(2,1)}, u32[]{:S(2)}, u32[]{:S(2)}) collective-permute-start(bf16[256,1024]{1,0:T(8,128)(2,1)} %collective-permute-done.18.rest_1_), channel_id=1, source_target_pairs={{2,4},{4,6},{3,5},{5,7},{10,12},{12,14},{11,13},{13,15},{18,20},{2... | collective-permute-start | bytes 1572872 | tf_op jit(solution)/shard_map/ppermute | solution.py:248
  136.2 0.9 add_convert_fusion.12
  137.2 1.4 collective-permute-start.16
  138.6 0.4 collective-permute-start.15
  139.0 1.1 collective-permute-done.22.rest_5_
  140.1 2.7 %collective-permute-start.29 = (bf16[256,1024]{1,0:T(8,128)(2,1)}, bf16[256,1024]{1,0:T(8,128)(2,1)}, u32[]{:S(2)}, u32[]{:S(2)}) collective-permute-start(bf16[256,1024]{1,0:T(8,128)(2,1)} %collective-permute-done.28.rest_5_), channel_id=1, source_target_pairs={{2,0},{3,1},{10,8},{11,9},{18,16},{19,17},{26,24},{27,25}} | collective-permute-start | bytes 1572872 | tf_op jit(solution)/shard_map/ppermute | solution.py:249
  142.8 1.5 collective-permute-start.26
  144.3 6.6 %collective-permute-done.17.rest_2_ = bf16[6,128,128]{2,1,0:T(8,128)(2,1)S(1)} collective-permute-done((bf16[6,128,128]{2,1,0:T(8,128)(2,1)}, bf16[6,128,128]{2,1,0:T(8,128)(2,1)S(1)}, u32[]{:S(2)}, u32[]{:S(2)}) %collective-permute-start.17) | collective-permute-done | bytes 196640 | tf_op jit(solution)/shard_map/ppermute | solution.py:164
  150.9 2.1 %collective-permute-start.23 = (bf16[256,1024]{1,0:T(8,128)(2,1)}, bf16[256,1024]{1,0:T(8,128)(2,1)}, u32[]{:S(2)}, u32[]{:S(2)}) collective-permute-start(bf16[256,1024]{1,0:T(8,128)(2,1)} %collective-permute-done.22.rest_5_), channel_id=1, source_target_pairs={{2,0},{3,1},{10,8},{11,9},{18,16},{19,17},{26,24},{27,25}} | collective-permute-start | bytes 1572872 | tf_op jit(solution)/shard_map/ppermute | solution.py:249
  153.0 1.4 collective-permute-start.20
  154.4 1.2 copy-done.1
  155.6 2.3 %shard_map.131 = (f32[2,128,1024]{2,1,0:T(8,128)}, f32[2,128,1024]{2,1,0:T(8,128)}) custom-call(s32[2]{0:T(128)S(1)} %pad_add_fusion.where_ref, f32[2,128,1024]{2,1,0:T(8,128)S(1)} %copy-done.1, bf16[6,128,640]{2,1,0:T(8,128)(2,1)S(1)} %fusion.23.left_ref, bf16[6,128,640]{2,1,0:T(8,128)(2,1)S(1)} %constant_dynamic-update-slice_fusion.right_ref, ...), custom_call_target="tpu_custom_call" | custom-call | tf_op jit(solution)/shard_map/pallas_call | solution.py:190
  157.9 3.8 %shard_map.132 = (f32[4,128,1024]{2,1,0:T(8,128)}, f32[4,128,1024]{2,1,0:T(8,128)}) custom-call(s32[2]{0:T(128)S(1)} %pad_add_fusion.where_ref, f32[4,128,1024]{2,1,0:T(8,128)S(1)} %copy-done, bf16[6,128,640]{2,1,0:T(8,128)(2,1)S(1)} %fusion.23.left_ref, bf16[6,128,640]{2,1,0:T(8,128)(2,1)S(1)} %constant_dynamic-update-slice_fusion.right_ref, ...), custom_call_target="tpu_custom_call" | custom-call | tf_op jit(solution)/shard_map/pallas_call | solution.py:190
  161.7 0.0 all-gather.2.cloned.1.call-done.a_ref
  161.8 2.3 %copy-done.6 = bf16[2,1024,1024]{2,1,0:T(8,128)(2,1)S(1)} copy-done((bf16[2,1024,1024]{2,1,0:T(8,128)(2,1)S(1)}, bf16[2,1024,1024]{2,1,0:T(8,128)(2,1)}, u32[]{:S(2)}) %copy-start.6) | copy-done | bytes 4194328
  164.0 12.4 %shard_map.133.left_ref = bf16[2048,2048]{1,0:T(8,128)(2,1)} custom-call(bf16[2,1024,1024]{2,1,0:T(8,128)(2,1)S(1)} %copy-done.6, bf16[2048,2048]{1,0:T(8,128)(2,1)} %w_ref.1), custom_call_target="tpu_custom_call" | custom-call | flops 8589934592 | bytes 20971520 | tf_op jit(solution)/shard_map/pallas_call | solution.py:227
  176.4 8.9 %shard_map.134.rest_7_ = bf16[2048,2048]{1,0:T(8,128)(2,1)} custom-call(s32[1]{0:T(128)} %bitcast.20.me_ref, bf16[2048,2048]{1,0:T(8,128)(2,1)} %shard_map.133.left_ref, bf16[256,1024]{1,0:T(8,128)(2,1)S(1)} %get-tuple-element.40.rest_0_, bf16[256,1024]{1,0:T(8,128)(2,1)S(1)} %copy-done.5, bf16[256,1024]{1,0:T(8,128)(2,1)} %collective-permute-done.25.rest_2_, ...), custom_call_target="tpu_custom_call" | custom-call | flops 4294967296 | bytes 10485760 | tf_op jit(solution)/shard_map/pallas_call | solution.py:289
  185.4 9.2 %shard_map.135 = bf16[2048,2048]{1,0:T(8,128)(2,1)} custom-call(s32[1]{0:T(128)} %bitcast.20.me_ref, bf16[2048,2048]{1,0:T(8,128)(2,1)} %shard_map.133.left_ref, bf16[256,1024]{1,0:T(8,128)(2,1)S(1)} %get-tuple-element.41.rest_0_, bf16[256,1024]{1,0:T(8,128)(2,1)} %collective-permute-done.18.rest_1_, ...), custom_call_target="tpu_custom_call", output_to_operand_aliasing={{}: (9, {})} | custom-call | flops 4294967296 | bytes 10485760 | tf_op jit(solution)/shard_map/pallas_call | solution.py:289
  (53 shorter events, 0.5 us)
Async XLA Ops:
  7.2 154.6 %all-gather.2.cloned.1.call-start = ((), (), s32[]{:S(2)}) async-start(), calls=%async_computation | async-start | bytes 4718592 | tf_op jit(solution)/shard_map/all_gather | solution.py:319
  8.0 0.7 copy-start.8
  8.7 13.3 %copy-start.7 = (f32[16,16]{1,0:T(8,128)S(1)}, f32[16,16]{1,0:T(8,128)}, u32[]{:S(2)}) copy-start(f32[16,16]{1,0:T(8,128)} %scale_ref.5) | copy-start | bytes 3076
  21.9 13.9 %copy-start.9 = (f32[16,32]{1,0:T(8,128)S(1)}, f32[16,32]{1,0:T(8,128)}, u32[]{:S(2)}) copy-start(f32[16,32]{1,0:T(8,128)} %scale_ref.4) | copy-start | bytes 6148
  21.9 33.3 %collective-permute-start = (bf16[2,4,128,640]{3,2,1,0:T(8,128)(2,1)S(1)}, bf16[2,4,128,640]{3,2,1,0:T(8,128)(2,1)S(1)}, u32[]{:S(2)}, u32[]{:S(2)}) collective-permute-start(bf16[2,4,128,640]{3,2,1,0:T(8,128)(2,1)S(1)} %get-tuple-element.16), channel_id=1, source_target_pairs={{0,1},{1,0},{2,3},{3,2},{4,5},{5,4},{6,7},{7,6},{8,9},{9,8},{10,11... | collective-permute-start | bytes 3932168 | tf_op jit(solution)/shard_map/ppermute | solution.py:128
  35.2 14.0 %copy-start.10 = (bf16[2,256,1024]{2,1,0:T(8,128)(2,1)S(1)}, bf16[2,256,1024]{2,1,0:T(8,128)(2,1)}, u32[]{:S(2)}) copy-start(bf16[2,256,1024]{2,1,0:T(8,128)(2,1)} %param.17) | copy-start | bytes 3145732
  35.3 22.3 %collective-permute-start.6 = (bf16[2,4,128,640]{3,2,1,0:T(8,128)(2,1)S(1)}, bf16[2,4,128,640]{3,2,1,0:T(8,128)(2,1)S(1)}, u32[]{:S(2)}, u32[]{:S(2)}) collective-permute-start(bf16[2,4,128,640]{3,2,1,0:T(8,128)(2,1)S(1)} %get-tuple-element.20), channel_id=1, source_target_pairs={{0,1},{1,0},{2,3},{3,2},{4,5},{5,4},{6,7},{7,6},{8,9},{9,8},{10,11... | collective-permute-start | bytes 3932168 | tf_op jit(solution)/shard_map/ppermute | solution.py:128
  49.0 10.8 %collective-permute-start.3 = (bf16[2,4,128,640]{3,2,1,0:T(8,128)(2,1)S(1)}, bf16[2,4,128,640]{3,2,1,0:T(8,128)(2,1)S(1)}, u32[]{:S(2)}, u32[]{:S(2)}) collective-permute-start(bf16[2,4,128,640]{3,2,1,0:T(8,128)(2,1)S(1)} %get-tuple-element.18), channel_id=1, source_target_pairs={{0,1},{1,0},{2,3},{3,2},{4,5},{5,4},{6,7},{7,6},{8,9},{9,8},{10,11... | collective-permute-start | bytes 3932168 | tf_op jit(solution)/shard_map/ppermute | solution.py:128
  49.3 58.0 %collective-permute-start.27 = (bf16[256,1024]{1,0:T(8,128)(2,1)S(1)}, bf16[256,1024]{1,0:T(8,128)(2,1)S(1)}, u32[]{:S(2)}, u32[]{:S(2)}) collective-permute-start(bf16[256,1024]{1,0:T(8,128)(2,1)S(1)} %get-tuple-element.40.rest_0_), channel_id=1, source_target_pairs={{2,0},{4,2},{6,4},{3,1},{5,3},{7,5},{10,8},{12,10},{14,12},{11,9},... | collective-permute-start | bytes 1572872 | tf_op jit(solution)/shard_map/ppermute | solution.py:249
  51.2 69.3 %collective-permute-start.24 = (bf16[256,1024]{1,0:T(8,128)(2,1)S(1)}, bf16[256,1024]{1,0:T(8,128)(2,1)S(1)}, u32[]{:S(2)}, u32[]{:S(2)}) collective-permute-start(bf16[256,1024]{1,0:T(8,128)(2,1)S(1)} %get-tuple-element.40.rest_0_), channel_id=1, source_target_pairs={{0,2},{2,4},{4,6},{1,3},{3,5},{5,7},{8,10},{10,12},{12,14},{9,11},... | collective-permute-start | bytes 1572872 | tf_op jit(solution)/shard_map/ppermute | solution.py:248
  55.2 67.3 %collective-permute-start.21 = (bf16[256,1024]{1,0:T(8,128)(2,1)S(1)}, bf16[256,1024]{1,0:T(8,128)(2,1)}, u32[]{:S(2)}, u32[]{:S(2)}) collective-permute-start(bf16[256,1024]{1,0:T(8,128)(2,1)S(1)} %get-tuple-element.41.rest_0_), channel_id=1, source_target_pairs={{2,0},{4,2},{6,4},{3,1},{5,3},{7,5},{10,8},{12,10},{14,12},{11,9},... | collective-permute-start | bytes 1572872 | tf_op jit(solution)/shard_map/ppermute | solution.py:249
  57.5 9.5 %collective-permute-start.1 = (bf16[2,128,640]{2,1,0:T(8,128)(2,1)S(1)}, bf16[2,128,640]{2,1,0:T(8,128)(2,1)S(1)}, u32[]{:S(2)}, u32[]{:S(2)}) collective-permute-start(bf16[2,128,640]{2,1,0:T(8,128)(2,1)S(1)} %get-tuple-element.35), channel_id=1, source_target_pairs={{0,8},{8,0},{16,24},{24,16},{1,9},{9,1},{17,25},{25,17},{2,10},{10... | collective-permute-start | bytes 983048 | tf_op jit(solution)/shard_map/ppermute | solution.py:123
  59.9 68.8 %collective-permute-start.18 = (bf16[256,1024]{1,0:T(8,128)(2,1)S(1)}, bf16[256,1024]{1,0:T(8,128)(2,1)}, u32[]{:S(2)}, u32[]{:S(2)}) collective-permute-start(bf16[256,1024]{1,0:T(8,128)(2,1)S(1)} %get-tuple-element.41.rest_0_), channel_id=1, source_target_pairs={{0,2},{2,4},{4,6},{1,3},{3,5},{5,7},{8,10},{10,12},{12,14},{9,11},... | collective-permute-start | bytes 1572872 | tf_op jit(solution)/shard_map/ppermute | solution.py:248
  67.0 8.5 %collective-permute-start.2 = (bf16[2,128,640]{2,1,0:T(8,128)(2,1)S(1)}, bf16[2,128,640]{2,1,0:T(8,128)(2,1)S(1)}, u32[]{:S(2)}, u32[]{:S(2)}) collective-permute-start(bf16[2,128,640]{2,1,0:T(8,128)(2,1)S(1)} %get-tuple-element.34), channel_id=1, source_target_pairs={{0,16},{8,24},{16,0},{24,8},{1,17},{9,25},{17,1},{25,9},{2,18},{10... | collective-permute-start | bytes 983048 | tf_op jit(solution)/shard_map/ppermute | solution.py:123
  75.6 7.7 %collective-permute-start.4 = (bf16[2,128,640]{2,1,0:T(8,128)(2,1)S(1)}, bf16[2,128,640]{2,1,0:T(8,128)(2,1)S(1)}, u32[]{:S(2)}, u32[]{:S(2)}) collective-permute-start(bf16[2,128,640]{2,1,0:T(8,128)(2,1)S(1)} %get-tuple-element.31), channel_id=1, source_target_pairs={{0,8},{8,0},{16,24},{24,16},{1,9},{9,1},{17,25},{25,17},{2,10},{10... | collective-permute-start | bytes 983048 | tf_op jit(solution)/shard_map/ppermute | solution.py:123
  83.3 7.1 %collective-permute-start.5 = (bf16[2,128,640]{2,1,0:T(8,128)(2,1)S(1)}, bf16[2,128,640]{2,1,0:T(8,128)(2,1)S(1)}, u32[]{:S(2)}, u32[]{:S(2)}) collective-permute-start(bf16[2,128,640]{2,1,0:T(8,128)(2,1)S(1)} %get-tuple-element.30), channel_id=1, source_target_pairs={{0,16},{8,24},{16,0},{24,8},{1,17},{9,25},{17,1},{25,9},{2,18},{10... | collective-permute-start | bytes 983048 | tf_op jit(solution)/shard_map/ppermute | solution.py:123
  90.4 7.1 %collective-permute-start.7 = (bf16[2,128,640]{2,1,0:T(8,128)(2,1)S(1)}, bf16[2,128,640]{2,1,0:T(8,128)(2,1)S(1)}, u32[]{:S(2)}, u32[]{:S(2)}) collective-permute-start(bf16[2,128,640]{2,1,0:T(8,128)(2,1)S(1)} %get-tuple-element.27), channel_id=1, source_target_pairs={{0,8},{8,0},{16,24},{24,16},{1,9},{9,1},{17,25},{25,17},{2,10},{10... | collective-permute-start | bytes 983048 | tf_op jit(solution)/shard_map/ppermute | solution.py:123
  97.4 8.8 %collective-permute-start.8 = (bf16[2,128,640]{2,1,0:T(8,128)(2,1)S(1)}, bf16[2,128,640]{2,1,0:T(8,128)(2,1)S(1)}, u32[]{:S(2)}, u32[]{:S(2)}) collective-permute-start(bf16[2,128,640]{2,1,0:T(8,128)(2,1)S(1)} %get-tuple-element.26), channel_id=1, source_target_pairs={{0,16},{8,24},{16,0},{24,8},{1,17},{9,25},{17,1},{25,9},{2,18},{10... | collective-permute-start | bytes 983048 | tf_op jit(solution)/shard_map/ppermute | solution.py:123
  106.3 8.9 %collective-permute-start.10 = (bf16[1,128,640]{2,1,0:T(8,128)(2,1)S(1)}, bf16[1,128,640]{2,1,0:T(8,128)(2,1)S(1)}, u32[]{:S(2)}, u32[]{:S(2)}) collective-permute-start(bf16[1,128,640]{2,1,0:T(8,128)(2,1)S(1)} %fusion.10), channel_id=1, source_target_pairs={{0,8},{8,0},{16,24},{24,16},{1,9},{9,1},{17,25},{25,17},{2,10},{10... | collective-permute-start | bytes 491528 | tf_op jit(solution)/shard_map/ppermute | solution.py:123
  107.3 29.8 %copy-start.2 = (bf16[256,1024]{1,0:T(8,128)(2,1)}, bf16[256,1024]{1,0:T(8,128)(2,1)S(1)}, u32[]{:S(2)}) copy-start(bf16[256,1024]{1,0:T(8,128)(2,1)S(1)} %collective-permute-done.27.rest_4_) | copy-start | bytes 1572868
  107.3 6.5 %collective-permute-start.9 = (bf16[1,128,640]{2,1,0:T(8,128)(2,1)S(1)}, bf16[1,128,640]{2,1,0:T(8,128)(2,1)S(1)}, u32[]{:S(2)}, u32[]{:S(2)}) collective-permute-start(bf16[1,128,640]{2,1,0:T(8,128)(2,1)S(1)} %fusion.11), channel_id=1, source_target_pairs={{0,16},{8,24},{16,0},{24,8},{1,17},{9,25},{17,1},{25,9},{2,18},{10... | collective-permute-start | bytes 491528 | tf_op jit(solution)/shard_map/ppermute | solution.py:123
  113.8 5.3 %collective-permute-start.11 = (bf16[1,128,640]{2,1,0:T(8,128)(2,1)S(1)}, bf16[1,128,640]{2,1,0:T(8,128)(2,1)S(1)}, u32[]{:S(2)}, u32[]{:S(2)}) collective-permute-start(bf16[1,128,640]{2,1,0:T(8,128)(2,1)S(1)} %fusion.9), channel_id=1, source_target_pairs={{0,16},{8,24},{16,0},{24,8},{1,17},{9,25},{17,1},{25,9},{2,18},{10... | collective-permute-start | bytes 491528 | tf_op jit(solution)/shard_map/ppermute | solution.py:123
  115.2 12.8 %collective-permute-start.12 = (bf16[1,128,640]{2,1,0:T(8,128)(2,1)S(1)}, bf16[1,128,640]{2,1,0:T(8,128)(2,1)S(1)}, u32[]{:S(2)}, u32[]{:S(2)}) collective-permute-start(bf16[1,128,640]{2,1,0:T(8,128)(2,1)S(1)} %fusion.8), channel_id=1, source_target_pairs={{0,8},{8,0},{16,24},{24,16},{1,9},{9,1},{17,25},{25,17},{2,10},{10... | collective-permute-start | bytes 491528 | tf_op jit(solution)/shard_map/ppermute | solution.py:123
  119.1 11.5 %collective-permute-start.13 = (bf16[1,128,640]{2,1,0:T(8,128)(2,1)S(1)}, bf16[1,128,640]{2,1,0:T(8,128)(2,1)S(1)}, u32[]{:S(2)}, u32[]{:S(2)}) collective-permute-start(bf16[1,128,640]{2,1,0:T(8,128)(2,1)S(1)} %fusion.7), channel_id=1, source_target_pairs={{0,16},{8,24},{16,0},{24,8},{1,17},{9,25},{17,1},{25,9},{2,18},{10... | collective-permute-start | bytes 491528 | tf_op jit(solution)/shard_map/ppermute | solution.py:123
  120.5 16.6 %copy-start.4 = (bf16[256,1024]{1,0:T(8,128)(2,1)}, bf16[256,1024]{1,0:T(8,128)(2,1)S(1)}, u32[]{:S(2)}) copy-start(bf16[256,1024]{1,0:T(8,128)(2,1)S(1)} %collective-permute-done.24.rest_1_) | copy-start | bytes 1572868
  120.5 16.6 %collective-permute-start.28 = (bf16[256,1024]{1,0:T(8,128)(2,1)S(1)}, bf16[256,1024]{1,0:T(8,128)(2,1)}, u32[]{:S(2)}, u32[]{:S(2)}) collective-permute-start(bf16[256,1024]{1,0:T(8,128)(2,1)S(1)} %collective-permute-done.27.rest_4_), channel_id=1, source_target_pairs={{2,0},{4,2},{3,1},{5,3},{10,8},{12,10},{11,9},{13,11},{18,16},{20,... | collective-permute-start | bytes 1572872 | tf_op jit(solution)/shard_map/ppermute | solution.py:249
  122.5 16.1 %collective-permute-start.25 = (bf16[256,1024]{1,0:T(8,128)(2,1)S(1)}, bf16[256,1024]{1,0:T(8,128)(2,1)}, u32[]{:S(2)}, u32[]{:S(2)}) collective-permute-start(bf16[256,1024]{1,0:T(8,128)(2,1)S(1)} %collective-permute-done.24.rest_1_), channel_id=1, source_target_pairs={{2,4},{4,6},{3,5},{5,7},{10,12},{12,14},{11,13},{13,15},{18,20},{2... | collective-permute-start | bytes 1572872 | tf_op jit(solution)/shard_map/ppermute | solution.py:248
  128.0 8.2 %collective-permute-start.14 = (bf16[1,128,640]{2,1,0:T(8,128)(2,1)S(1)}, bf16[1,128,640]{2,1,0:T(8,128)(2,1)S(1)}, u32[]{:S(2)}, u32[]{:S(2)}) collective-permute-start(bf16[1,128,640]{2,1,0:T(8,128)(2,1)S(1)} %fusion.6), channel_id=1, source_target_pairs={{0,8},{8,0},{16,24},{24,16},{1,9},{9,1},{17,25},{25,17},{2,10},{10... | collective-permute-start | bytes 491528 | tf_op jit(solution)/shard_map/ppermute | solution.py:123
  128.7 11.4 %collective-permute-start.22 = (bf16[256,1024]{1,0:T(8,128)(2,1)}, bf16[256,1024]{1,0:T(8,128)(2,1)}, u32[]{:S(2)}, u32[]{:S(2)}) collective-permute-start(bf16[256,1024]{1,0:T(8,128)(2,1)} %collective-permute-done.21.rest_4_), channel_id=1, source_target_pairs={{2,0},{4,2},{3,1},{5,3},{10,8},{12,10},{11,9},{13,11},{18,16},{20,... | collective-permute-start | bytes 1572872 | tf_op jit(solution)/shard_map/ppermute | solution.py:249
  130.7 12.2 %collective-permute-start.19 = (bf16[256,1024]{1,0:T(8,128)(2,1)}, bf16[256,1024]{1,0:T(8,128)(2,1)}, u32[]{:S(2)}, u32[]{:S(2)}) collective-permute-start(bf16[256,1024]{1,0:T(8,128)(2,1)} %collective-permute-done.18.rest_1_), channel_id=1, source_target_pairs={{2,4},{4,6},{3,5},{5,7},{10,12},{12,14},{11,13},{13,15},{18,20},{2... | collective-permute-start | bytes 1572872 | tf_op jit(solution)/shard_map/ppermute | solution.py:248
  137.2 13.7 %collective-permute-start.17 = (bf16[6,128,128]{2,1,0:T(8,128)(2,1)}, bf16[6,128,128]{2,1,0:T(8,128)(2,1)S(1)}, u32[]{:S(2)}, u32[]{:S(2)}) collective-permute-start(bf16[6,128,128]{2,1,0:T(8,128)(2,1)} %get-tuple-element.37), channel_id=1, source_target_pairs={{0,9},{1,16},{8,17},{9,24},{16,25},{17,0},{24,1},{25,8},{2,11},{3,... | collective-permute-start | bytes 589832 | tf_op jit(solution)/shard_map/ppermute | solution.py:164
  137.2 15.8 %collective-permute-start.16 = (bf16[6,128,128]{2,1,0:T(8,128)(2,1)}, bf16[6,128,128]{2,1,0:T(8,128)(2,1)S(1)}, u32[]{:S(2)}, u32[]{:S(2)}) collective-permute-start(bf16[6,128,128]{2,1,0:T(8,128)(2,1)} %get-tuple-element.38), channel_id=1, source_target_pairs={{0,8},{1,9},{8,16},{9,17},{16,24},{17,25},{24,0},{25,1},{2,10},{3,... | collective-permute-start | bytes 589832 | tf_op jit(solution)/shard_map/ppermute | solution.py:164
  138.6 15.8 %collective-permute-start.15 = (bf16[6,128,128]{2,1,0:T(8,128)(2,1)}, bf16[6,128,128]{2,1,0:T(8,128)(2,1)}, u32[]{:S(2)}, u32[]{:S(2)}) collective-permute-start(bf16[6,128,128]{2,1,0:T(8,128)(2,1)} %get-tuple-element.39), channel_id=1, source_target_pairs={{0,1},{1,8},{8,9},{9,16},{16,17},{17,24},{24,25},{25,0},{2,3},{3,1... | collective-permute-start | bytes 589832 | tf_op jit(solution)/shard_map/ppermute | solution.py:164
  139.0 18.9 %copy-start = (f32[4,128,1024]{2,1,0:T(8,128)S(1)}, f32[4,128,1024]{2,1,0:T(8,128)}, u32[]{:S(2)}) copy-start(f32[4,128,1024]{2,1,0:T(8,128)} %prior_ref.3) | copy-start | bytes 6291460
  140.1 36.3 %collective-permute-start.29 = (bf16[256,1024]{1,0:T(8,128)(2,1)}, bf16[256,1024]{1,0:T(8,128)(2,1)}, u32[]{:S(2)}, u32[]{:S(2)}) collective-permute-start(bf16[256,1024]{1,0:T(8,128)(2,1)} %collective-permute-done.28.rest_5_), channel_id=1, source_target_pairs={{2,0},{3,1},{10,8},{11,9},{18,16},{19,17},{26,24},{27,25}} | collective-permute-start | bytes 1572872 | tf_op jit(solution)/shard_map/ppermute | solution.py:249
  142.8 33.6 %collective-permute-start.26 = (bf16[256,1024]{1,0:T(8,128)(2,1)}, bf16[256,1024]{1,0:T(8,128)(2,1)}, u32[]{:S(2)}, u32[]{:S(2)}) collective-permute-start(bf16[256,1024]{1,0:T(8,128)(2,1)} %collective-permute-done.25.rest_2_), channel_id=1, source_target_pairs={{4,6},{5,7},{12,14},{13,15},{20,22},{21,23},{28,30},{29,31}} | collective-permute-start | bytes 1572872 | tf_op jit(solution)/shard_map/ppermute | solution.py:248
  150.9 34.5 %collective-permute-start.23 = (bf16[256,1024]{1,0:T(8,128)(2,1)}, bf16[256,1024]{1,0:T(8,128)(2,1)}, u32[]{:S(2)}, u32[]{:S(2)}) collective-permute-start(bf16[256,1024]{1,0:T(8,128)(2,1)} %collective-permute-done.22.rest_5_), channel_id=1, source_target_pairs={{2,0},{3,1},{10,8},{11,9},{18,16},{19,17},{26,24},{27,25}} | collective-permute-start | bytes 1572872 | tf_op jit(solution)/shard_map/ppermute | solution.py:249
  153.0 32.4 %collective-permute-start.20 = (bf16[256,1024]{1,0:T(8,128)(2,1)}, bf16[256,1024]{1,0:T(8,128)(2,1)}, u32[]{:S(2)}, u32[]{:S(2)}) collective-permute-start(bf16[256,1024]{1,0:T(8,128)(2,1)} %collective-permute-done.19.rest_2_), channel_id=1, source_target_pairs={{4,6},{5,7},{12,14},{13,15},{20,22},{21,23},{28,30},{29,31}} | collective-permute-start | bytes 1572872 | tf_op jit(solution)/shard_map/ppermute | solution.py:248
  154.4 1.2 copy-start.1
  161.7 14.7 %copy-start.3 = (bf16[256,1024]{1,0:T(8,128)(2,1)S(1)}, bf16[256,1024]{1,0:T(8,128)(2,1)}, u32[]{:S(2)}) copy-start(bf16[256,1024]{1,0:T(8,128)(2,1)} %copy-done.2) | copy-start | bytes 1572868
  161.7 14.7 %copy-start.5 = (bf16[256,1024]{1,0:T(8,128)(2,1)S(1)}, bf16[256,1024]{1,0:T(8,128)(2,1)}, u32[]{:S(2)}) copy-start(bf16[256,1024]{1,0:T(8,128)(2,1)} %copy-done.4) | copy-start | bytes 1572868
  161.8 2.3 %copy-start.6 = (bf16[2,1024,1024]{2,1,0:T(8,128)(2,1)S(1)}, bf16[2,1024,1024]{2,1,0:T(8,128)(2,1)}, u32[]{:S(2)}) copy-start(bf16[2,1024,1024]{2,1,0:T(8,128)(2,1)} %all-gather.2.cloned.1.call-done.a_ref) | copy-start | bytes 12582916
Sparse Core Ops, SparseCore 0:
  9.9 37.8 all-gather.1
